TPU v7x, 512 devices: a whole 4x4x16 slice. The times are simulated.
512 devices in a mesh: dp: 64 (over z_lo, y, core), seq: 8 (over z_hi, x).
Axes of the slice: x: 4, y: 4, z: 16 (z_hi: 2, z_lo: 8; z = z_hi * 8 + z_lo), core: 2. Of those that a mesh axis runs over, the one named last changes fastest.
Arguments:
- hidden_in: bfloat16 [65536, 2048], P(('dp', 'seq')), may hold values from -6 to 6
- norm_gain: float32 [2048], replicated, may hold values from 0.5 to 1.5
- resid_grad: bfloat16 [65536, 2048], P(('dp', 'seq')), may hold values from -3 to 3
- key_output_gradient: bfloat16 [65536, 512], P('dp', 'seq'), may hold values from -6 to 6
- value_output_gradient: bfloat16 [65536, 512], P('dp', 'seq'), may hold values from -6 to 6
- key_matrix: bfloat16 [2048, 512], P(None, 'seq'), may hold values from -0.125 to 0.125
- value_matrix: bfloat16 [2048, 512], P(None, 'seq'), may hold values from -0.125 to 0.125
Outputs:
- input_grad: bfloat16 [65536, 2048], P(('dp', 'seq'))
- key_weight_grad: float32 [2048, 512], P('dp', 'seq')
- value_weight_grad: float32 [2048, 512], P('dp', 'seq')
- gain_grad: float32 [2048], replicated
All inputs are finite; a program needn't handle non-finite values.
Results may differ from a plain program's by a relative error of at most 0.0029.
Values may be sent and summed in bfloat16 or wider, within the bound.
A program may use at most 64 MiB of HBM per device.

v0:
```python
import math

import jax
import jax.numpy as jnp
from jax import lax
from jax.sharding import PartitionSpec as P

EPSILON = 1e-05


def normalize(rows, norm_gain):
    widened = rows.astype(jnp.float32)
    inv_rms = lax.rsqrt(jnp.mean(widened * widened, axis=-1, keepdims=True) + EPSILON)
    unit_rows = widened * inv_rms
    return (inv_rms, unit_rows, (unit_rows * norm_gain).astype(jnp.bfloat16))


def per_device(
    hidden_in,
    norm_gain,
    resid_grad,
    key_output_gradient,
    value_output_gradient,
    key_matrix,
    value_matrix,
):
    total_tokens = key_output_gradient.shape[0] * lax.axis_size("dp")
    scale = 1.0 / math.sqrt(total_tokens)
    inv_rms, unit_rows, normed = normalize(hidden_in, norm_gain)
    normed_piece = lax.all_gather(normed, "seq", axis=0, tiled=True)
    key_next = jnp.einsum(
        "td,tc->dc", normed_piece, key_output_gradient, preferred_element_type=jnp.float32
    )
    value_next = jnp.einsum(
        "td,tc->dc", normed_piece, value_output_gradient, preferred_element_type=jnp.float32
    )
    key_sum, value_sum = (
        lax.psum_scatter(key_next, "dp", scatter_dimension=0, tiled=True),
        lax.psum_scatter(value_next, "dp", scatter_dimension=0, tiled=True),
    )
    key_tok, value_tok = (
        lax.all_to_all(key_output_gradient, "seq", split_axis=0, concat_axis=1, tiled=True),
        lax.all_to_all(value_output_gradient, "seq", split_axis=0, concat_axis=1, tiled=True),
    )
    normed_grad = jnp.einsum(
        "tc,dc->td",
        key_tok,
        lax.all_gather(key_matrix, "seq", axis=1, tiled=True),
        preferred_element_type=jnp.float32,
    )
    normed_grad = normed_grad + jnp.einsum(
        "tc,dc->td",
        value_tok,
        lax.all_gather(value_matrix, "seq", axis=1, tiled=True),
        preferred_element_type=jnp.float32,
    )
    gain_total = lax.psum(jnp.sum(normed_grad * unit_rows, axis=0), ("dp", "seq"))
    scaled = normed_grad * norm_gain
    inner = jnp.mean(scaled * unit_rows, axis=-1, keepdims=True)
    input_grad = (resid_grad.astype(jnp.float32) + inv_rms * (scaled - unit_rows * inner)).astype(
        jnp.bfloat16
    )
    return (input_grad, key_sum * scale, value_sum * scale, gain_total * scale)


def solution(mesh):
    return jax.shard_map(
        per_device,
        mesh=mesh,
        in_specs=(
            P(("dp", "seq"), None),
            P(),
            P(("dp", "seq"), None),
            P("dp", "seq"),
            P("dp", "seq"),
            P(None, "seq"),
            P(None, "seq"),
        ),
        out_specs=(P(("dp", "seq"), None), P("dp", "seq"), P("dp", "seq"), P()),
        check_vma=False,
    )
```

profile of v0, /device:TPU:1, one launch (start us, length us, event | category | flops | bytes accessed | tf_op | source)
XLA Modules:
  0.0 1289.4 jit_solution(17817953286696897681)
XLA Ops:
  7.2 0.0 copy-start
  7.2 0.0 all-gather.4.cloned.1.call-start
  7.2 0.7 all-gather.4.cloned.1.call-update
  7.9 0.0 all-gather.6.cloned.1.call-start
  8.0 0.7 all-gather.6.cloned.1.call-update
  8.7 1.6 copy_bitcast_fusion.1
  10.2 18.1 %all-to-all-start = ((bf16[8,128,64]{1,2,0:T(8,128)(2,1)}), bf16[8,128,64]{1,2,0:T(8,128)(2,1)S(1)}, u32[]{:S(2)}, u32[]{:S(2)}) async-start(bf16[8,128,64]{1,2,0:T(8,128)(2,1)} %copy_bitcast_fusion.1), calls=%async_computation | async-start | bytes 262144 | tf_op jit(solution)/shard_map/all_to_all | solution.py:42
  28.3 0.0 copy-start.1
  28.4 0.0 copy-start.4
  28.4 1.3 fusion.11
  29.7 0.0 copy-done
  29.7 0.7 copy_bitcast_fusion
  30.3 12.2 all-to-all-done
  42.5 3.4 all-to-all-start.1
  45.9 0.0 all-gather.8.cloned.1.call-start
  45.9 90.2 %all-gather.4.cloned.1.call-done = bf16[2048,512]{0,1:T(8,128)(2,1)} async-done(((bf16[2048,64]{0,1:T(8,128)(2,1)}), bf16[2048,512]{0,1:T(8,128)(2,1)}) %all-gather.4.cloned.1.call-update) | async-done | bytes 2097168 | tf_op jit(solution)/shard_map/all_gather | solution.py:48
  136.1 2.1 fusion.12
  138.2 0.0 all-to-all-done.1
  138.2 112.4 %all-gather.6.cloned.1.call-done = bf16[2048,512]{0,1:T(8,128)(2,1)} async-done(((bf16[2048,64]{0,1:T(8,128)(2,1)}), bf16[2048,512]{0,1:T(8,128)(2,1)}) %all-gather.6.cloned.1.call-update) | async-done | bytes 2097168 | tf_op jit(solution)/shard_map/all_gather | solution.py:54
  250.6 0.0 copy-done.1
  250.6 0.0 copy-done.4
  250.6 3.0 fusion.10
  253.6 0.0 all-gather.8.cloned.1.call-update
  253.6 0.0 copy-start.3
  253.6 0.0 reduce-scatter.5.cloned.1.call-start
  253.7 173.8 %all-gather.8.cloned.1.call-done = bf16[1024,2048]{1,0:T(8,128)(2,1)} async-done(((bf16[128,2048]{1,0:T(8,128)(2,1)}), bf16[1024,2048]{1,0:T(8,128)(2,1)}) %all-gather.8.cloned.1.call-update) | async-done | bytes 4194320 | tf_op jit(solution)/shard_map/all_gather | solution.py:30
  427.5 4.5 fusion.14
  431.9 0.0 reduce-scatter.5.cloned.1.call-update
  432.0 0.0 copy-start.2
  432.0 0.0 reduce-scatter.3.cloned.1.call-start
  432.0 0.0 copy-done.3
  432.0 4.5 fusion.13
  436.5 0.0 reduce-scatter.3.cloned.1.call-update
  436.6 100.6 %psum.7 = f32[2048]{0:T(1024)S(1)} all-reduce(f32[2048]{0:T(1024)S(1)} %get-tuple-element.4), channel_id=1, replica_groups=mesh['dp'=64,'seq'=8] {'dp','seq'}, use_global_device_ids=true, to_apply=%region_5.0 | all-reduce | flops 2048 | bytes 16384 | tf_op jit(solution)/shard_map/psum | solution.py:57
  537.1 0.6 broadcast_multiply_fusion.2
  537.7 0.0 copy-done.2
  537.7 1.2 fusion.8
  538.9 311.7 %reduce-scatter.5.cloned.1.call-done = f32[32,64]{1,0:T(8,128)} async-done(((f32[2048,64]{1,0:T(8,128)}), f32[32,64]{1,0:T(8,128)}) %reduce-scatter.5.cloned.1.call-update) | async-done | bytes 8208 | tf_op jit(solution)/shard_map/reduce_scatter | solution.py:39
  850.6 1.3 broadcast_multiply_fusion
  851.9 429.6 %reduce-scatter.3.cloned.1.call-done = f32[32,64]{1,0:T(8,128)} async-done(((f32[2048,64]{1,0:T(8,128)}), f32[32,64]{1,0:T(8,128)}) %reduce-scatter.3.cloned.1.call-update) | async-done | bytes 8208 | tf_op jit(solution)/shard_map/reduce_scatter | solution.py:38
  1281.5 1.3 broadcast_multiply_fusion.1
  (2 shorter events, 0.0 us)
Async XLA Ops:
  7.2 22.5 %copy-start = (bf16[1024,64]{0,1:T(8,128)(2,1)S(1)}, bf16[1024,64]{0,1:T(8,128)(2,1)}, u32[]{:S(2)}) copy-start(bf16[1024,64]{0,1:T(8,128)(2,1)} %param.11) | copy-start | bytes 393220
  7.2 129.0 %all-gather.4.cloned.1.call-start = ((), (), s32[]{:S(2)}) async-start(), calls=%async_computation.4 | async-start | bytes 2359296 | tf_op jit(solution)/shard_map/all_gather | solution.py:48
  7.9 242.7 %all-gather.6.cloned.1.call-start = ((), (), s32[]{:S(2)}) async-start(), calls=%async_computation.5 | async-start | bytes 2359296 | tf_op jit(solution)/shard_map/all_gather | solution.py:54
  10.2 32.2 %all-to-all-start = ((bf16[8,128,64]{1,2,0:T(8,128)(2,1)}), bf16[8,128,64]{1,2,0:T(8,128)(2,1)S(1)}, u32[]{:S(2)}, u32[]{:S(2)}) async-start(bf16[8,128,64]{1,2,0:T(8,128)(2,1)} %copy_bitcast_fusion.1), calls=%async_computation | async-start | bytes 262144 | tf_op jit(solution)/shard_map/all_to_all | solution.py:42
  28.3 222.2 %copy-start.1 = (bf16[128,2048]{1,0:T(8,128)(2,1)S(1)}, bf16[128,2048]{1,0:T(8,128)(2,1)}, u32[]{:S(2)}) copy-start(bf16[128,2048]{1,0:T(8,128)(2,1)} %param.7) | copy-start | bytes 1572868
  28.4 222.2 %copy-start.4 = (f32[2048]{0:T(1024)S(1)}, f32[2048]{0:T(1024)}, u32[]{:S(2)}) copy-start(f32[2048]{0:T(1024)} %param.8) | copy-start | bytes 24580
  42.5 95.7 %all-to-all-start.1 = ((bf16[8,128,64]{1,2,0:T(8,128)(2,1)}), bf16[8,128,64]{1,2,0:T(8,128)(2,1)S(1)}, u32[]{:S(2)}, u32[]{:S(2)}) async-start(bf16[8,128,64]{1,2,0:T(8,128)(2,1)} %copy_bitcast_fusion), calls=%async_computation.1 | async-start | bytes 262144 | tf_op jit(solution)/shard_map/all_to_all | solution.py:43
  45.9 381.6 %all-gather.8.cloned.1.call-start = ((), (), s32[]{:S(2)}) async-start(), calls=%async_computation.6 | async-start | bytes 4718592 | tf_op jit(solution)/shard_map/all_gather | solution.py:30
  253.6 178.4 %copy-start.3 = (bf16[1024,64]{0,1:T(8,128)(2,1)S(1)}, bf16[1024,64]{0,1:T(8,128)(2,1)}, u32[]{:S(2)}) copy-start(bf16[1024,64]{0,1:T(8,128)(2,1)} %param.10) | copy-start | bytes 393220
  253.6 597.0 %reduce-scatter.5.cloned.1.call-start = ((), (), s32[]{:S(2)}) async-start(), calls=%async_computation.8 | async-start | bytes 1064960 | tf_op jit(solution)/shard_map/reduce_scatter | solution.py:39
  432.0 105.8 %copy-start.2 = (bf16[128,2048]{1,0:T(8,128)(2,1)S(1)}, bf16[128,2048]{1,0:T(8,128)(2,1)}, u32[]{:S(2)}) copy-start(bf16[128,2048]{1,0:T(8,128)(2,1)} %param.9) | copy-start | bytes 1572868
  432.0 849.5 %reduce-scatter.3.cloned.1.call-start = ((), (), s32[]{:S(2)}) async-start(), calls=%async_computation.7 | async-start | bytes 1064960 | tf_op jit(solution)/shard_map/reduce_scatter | solution.py:38
Sparse Core Ops, SparseCore 0:
  11.2 124.8 all-gather.3
  139.3 111.1 all-gather.5
  254.4 173.0 all-gather.7
  432.1 418.4 reduce-scatter.4
  853.5 428.0 reduce-scatter.2
where the time goes:
time: 1300 us; the launch traced here: 1290 us
  waiting for transfers between devices  1130 us (87%)
  blocking collectives  101 us (8%)
  starting transfers between devices  21.7 us (2%)
  matrix products  14.1 us (1%)
  between operations  13.9 us (1%)
    reduce_scatter x1, waiting for transfers between devices, per_device(): lax.psum_scatter(key_next, 'dp', scatter_dimension=0, tiled=True)  430 us
    reduce_scatter x1, waiting for transfers between devices, per_device(): lax.psum_scatter(value_next, 'dp', scatter_dimension=0, tiled=True)  312 us
    all_gather x1, waiting for transfers between devices, per_device(): normed_piece = lax.all_gather(normed, 'seq', axis=0, tiled=True)  174 us
    all_gather x1, waiting for transfers between devices, per_device(): lax.all_gather(value_matrix, 'seq', axis=1, tiled=True)  112 us
    psum x1, blocking collectives, per_device(): lax.psum(jnp.sum(normed_grad * unit_rows, axis=0), ('dp', 'seq'))  101 us
    all_gather x1, waiting for transfers between devices, per_device(): lax.all_gather(key_matrix, 'seq', axis=1, tiled=True)  90.2 us
  transfers between devices with their start and end apart: 7, of which 6 were waited for; matrix products, arithmetic and copies ran while one was open for 1% of the time, Pallas kernels for 0%

commit v1 on v0

v1 whole, which is shorter than its diff:
```python
import functools
import math

import jax
import jax.numpy as jnp
from jax import lax
from jax.experimental import pallas as pl
from jax.experimental.pallas import tpu as pltpu
from jax.sharding import PartitionSpec as P

EPSILON = 1e-05
MESH = pl.DeviceIdType.MESH
BF16, F32 = jnp.bfloat16, jnp.float32
NX, NY, NZL, NZH, NC = 4, 4, 8, 2, 2
NT_DIMS = (((1,), (1,)), ((), ()))


def kernel(
    scale,
    hid_hbm,
    gain_hbm,
    res_hbm,
    kt_hbm,
    vt_hbm,
    wk_hbm,
    wv_hbm,
    out_ref,
    kw_ref,
    vw_ref,
    gain_out,
    hid,
    res,
    gain,
    inv_ref,
    nrm,
    nt,
    ng_all,
    kv,
    kv_far,
    kv_tok,
    w_all,
    normed_grad,
    y_send,
    y_recv,
    own_sum,
    z_send,
    z_recv,
    ga,
    g1,
    g2,
    g3,
    gf,
    load_sem,
    wz_s,
    wz_r,
    wx_s,
    wx_r,
    wy_s,
    wy_r,
    wc_s,
    wc_r,
    kz_s,
    kz_r,
    kc_s,
    kc_r,
    kx_s,
    kx_r,
    n_s,
    n_r,
    y_s,
    y_r,
    z_s,
    z_r,
    g1_s,
    g1_r,
    g2_s,
    g2_r,
    g3_s,
    g3_r,
    g4_s,
    g4_r,
):
    dp, sq = lax.axis_index("dp"), lax.axis_index("seq")
    c, y, zl = dp % NC, (dp // NC) % NY, dp // (NC * NY)
    x, zh = sq % NX, sq // NX
    z = zh * NZL + zl
    nz = NZL * NZH
    rows, width = hid.shape
    cols = wk_hbm.shape[0]
    half = rows * NX
    piece = width // (NY * NC)

    def device(dc=0, dx=0, dy=0, zz=None):
        cc, xx, yy = (c + dc) % NC, (x + dx) % NX, (y + dy) % NY
        zz = z if zz is None else zz
        return ((zz % NZL) * NY + yy) * NC + cc, (zz // NZL) * NX + xx

    def remote(src, dst, ssem, rsem, to):
        return pltpu.make_async_remote_copy(
            src_ref=src, dst_ref=dst, send_sem=ssem, recv_sem=rsem, device_id=to, device_id_type=MESH
        )

    def aligned(index, size):
        return pl.ds(pl.multiple_of(index * size, size), size)

    near, far = aligned(zh, half), aligned(1 - zh, half)
    loads = [
        pltpu.make_async_copy(hid_hbm, hid, load_sem.at[0]),
        pltpu.make_async_copy(gain_hbm, gain, load_sem.at[1]),
        pltpu.make_async_copy(kt_hbm.at[:, far], kv_far.at[pl.ds(0, cols)], load_sem.at[2]),
        pltpu.make_async_copy(vt_hbm.at[:, far], kv_far.at[pl.ds(cols, cols)], load_sem.at[3]),
        pltpu.make_async_copy(wk_hbm, w_all.at[0, pl.ds(0, cols)], load_sem.at[4]),
        pltpu.make_async_copy(wv_hbm, w_all.at[0, pl.ds(cols, cols)], load_sem.at[5]),
        pltpu.make_async_copy(kt_hbm.at[:, near], kv.at[0, pl.ds(0, cols)], load_sem.at[6]),
        pltpu.make_async_copy(vt_hbm.at[:, near], kv.at[0, pl.ds(cols, cols)], load_sem.at[7]),
        pltpu.make_async_copy(res_hbm, res, load_sem.at[8]),
    ]
    for load in loads:
        load.start()

    barrier = pltpu.get_barrier_semaphore()
    xc = [(dx, dc) for dx in range(NX) for dc in range(NC) if dx or dc]
    peers = [device(dc=dc, dx=dx) for dx, dc in xc]
    peers += [device(dy=dy) for dy in range(1, NY)]
    peers += [device(zz=(z + dz) % nz) for dz in range(1, nz)]
    for peer in peers:
        pl.semaphore_signal(barrier, inc=1, device_id=peer, device_id_type=MESH)

    loads[0].wait()
    loads[1].wait()
    step = 16
    for at in range(0, rows, step):
        wide = hid[at : at + step].astype(F32)
        inv = lax.rsqrt(jnp.mean(wide * wide, axis=-1, keepdims=True) + EPSILON)
        inv_ref[at : at + step] = inv
        nrm[at : at + step] = (wide * inv * gain[...]).astype(BF16)
    block = width // (NC * NY * NZL)
    lane = min(128, width)
    for at in range(0, width, lane):
        turned = nrm[:, at : at + lane].T
        for part in range(lane // block):
            b = at // block + part
            bc, by, bz = b % NC, (b // NC) % NY, b // (NC * NY)
            nt[bc, by, bz * block : (bz + 1) * block] = turned[part * block : (part + 1) * block]
    for load in loads[2:8]:
        load.wait()
    pl.semaphore_wait(barrier, len(peers))

    q = aligned(c * NY + y, piece)
    sends = []

    def go(copy):
        copy.start()
        sends.append(copy)
        return copy

    w_z = go(remote(w_all.at[0, :, q], w_all.at[NX, :, q], wz_s, wz_r, device(zz=nz - 1 - z)))
    k_z = go(remote(kv_far, kv.at[0, pl.ds(2 * cols, 2 * cols)], kz_s, kz_r, device(zz=(z + nz // 2) % nz)))
    w_x = [
        go(remote(w_all.at[0, :, q], w_all.at[dx, :, q], wx_s.at[dx - 1], wx_r.at[dx - 1], device(dx=dx)))
        for dx in range(1, NX)
    ]
    k_c = go(remote(kv.at[0, pl.ds(0, 2 * cols)], kv.at[1, pl.ds(0, 2 * cols)], kc_s.at[0], kc_r.at[0], device(dc=1)))

    def token_sends(rel):
        return [
            go(
                remote(
                    kv.at[0, pl.ds(rel * 2 * cols, 2 * cols), aligned((x + dx) % NX, rows)],
                    kv_tok.at[rel * NX + dx],
                    kx_s.at[rel * NX + dx],
                    kx_r.at[rel * NX + dx],
                    device(dx=dx),
                )
            )
            for dx in range(1, NX)
        ]

    k_x = token_sends(0)
    mine = aligned(x, rows)
    n_all = []
    for i, (dx, dc) in enumerate(xc):
        n_all.append(
            go(remote(nt.at[(c + dc) % NC], ng_all.at[dc, :, :, mine], n_s.at[i], n_r.at[i], device(dc=dc, dx=dx)))
        )
    own = pltpu.make_async_copy(nt.at[c], ng_all.at[0, :, :, mine], load_sem.at[9])
    own.start()

    def y_sends(first, count, rel):
        return [
            go(
                remote(
                    w_all.at[pl.ds(first, count), :, q],
                    w_all.at[pl.ds(first, count), :, q],
                    wy_s.at[rel * NY + dy],
                    wy_r.at[rel * NY + dy],
                    device(dy=dy),
                )
            )
            for dy in range(1, NY)
        ]

    for copy in w_x:
        copy.wait_recv()
    w_y = y_sends(1, NX - 1, 0)
    w_z.wait_recv()
    w_x2 = [
        go(
            remote(
                w_all.at[NX, :, q],
                w_all.at[NX + dx, :, q],
                wx_s.at[NX - 1 + dx - 1],
                wx_r.at[NX - 1 + dx - 1],
                device(dx=dx),
            )
        )
        for dx in range(1, NX)
    ]
    for copy in w_x2:
        copy.wait_recv()
    w_y2 = y_sends(NX, NX, 1)

    k_z.wait_recv()
    k_c2 = go(
        remote(
            kv.at[0, pl.ds(2 * cols, 2 * cols)],
            kv.at[1, pl.ds(2 * cols, 2 * cols)],
            kc_s.at[1],
            kc_r.at[1],
            device(dc=1),
        )
    )
    k_x += token_sends(1)
    own.wait()
    for copy in n_all:
        copy.wait_recv()
    k_c.wait_recv()
    k_c2.wait_recv()

    y_all = []
    for dy in [d for d in (2, 1, 3, 0) if d < NY]:
        to = (y + dy) % NY
        total = lax.dot_general(ng_all[0, to], kv[0], NT_DIMS, preferred_element_type=F32)
        total = total + lax.dot_general(ng_all[1, to], kv[1], NT_DIMS, preferred_element_type=F32)
        if dy:
            y_send[dy - 1] = total.astype(BF16)
            y_all.append(go(remote(y_send.at[dy - 1], y_recv.at[dy - 1], y_s.at[dy - 1], y_r.at[dy - 1], device(dy=dy))))
        else:
            own_sum[...] = total

    side = aligned(c, width // NC)
    for copy in w_y + w_y2:
        copy.wait_recv()
    w_c = go(
        remote(w_all.at[pl.ds(1, 2 * NX - 1), :, side], w_all.at[pl.ds(1, 2 * NX - 1), :, side], wc_s, wc_r, device(dc=1))
    )

    for copy in y_all:
        copy.wait_recv()
    total = own_sum[...]
    for i in range(NY - 1):
        total = total + y_recv[i].astype(F32)
    own_sum[...] = total
    for rel in range(NZH):
        z_send[rel] = total[:, rel * 2 * cols : (rel + 1) * 2 * cols].astype(BF16)
    z_all = []
    for dz in sorted(range(1, nz), key=lambda d: -min(d, nz - d)):
        to = (z + dz) % nz
        z_all.append(
            go(
                remote(
                    z_send.at[(to // NZL + zh) % NZH, aligned(to % NZL, block)],
                    z_recv.at[dz - 1],
                    z_s.at[dz - 1],
                    z_r.at[dz - 1],
                    device(zz=to),
                )
            )
        )

    for copy in k_x:
        copy.wait_recv()
    for rel in range(NZH):
        kv_tok[rel * NX] = kv[0, rel * 2 * cols : (rel + 1) * 2 * cols, mine]
    w_c.wait_recv()
    tok = kv_tok[...].reshape(-1, rows).T
    inner = jnp.zeros((rows, 1), F32)
    inv = inv_ref[...]
    chunk = min(256, width)
    for at in range(0, width, chunk):
        here = slice(at, at + chunk)
        weights = w_all[:, :, here].reshape(-1, chunk)
        grad = jnp.dot(tok, weights, preferred_element_type=F32)
        unit = hid[:, here].astype(F32) * inv
        normed_grad[:, here] = grad
        both = grad * unit
        inner = inner + jnp.sum(both * gain[:, here], axis=-1, keepdims=True)
        total = jnp.sum(both, axis=0, keepdims=True)
        part = width // (NX * NC)
        for i in range(chunk // part):
            ga[at // part + i] = total[:, i * part : (i + 1) * part]
    inner = inner * (1.0 / width)

    g_1 = []
    me = x * NC + c
    for i, (dx, dc) in enumerate(xc):
        to = ((x + dx) % NX) * NC + (c + dc) % NC
        g_1.append(go(remote(ga.at[to], g1.at[me], g1_s.at[i], g1_r.at[i], device(dc=dc, dx=dx))))
    g1[me] = ga[me]

    loads[8].wait()
    for at in range(0, width, chunk):
        here = slice(at, at + chunk)
        unit = hid[:, here].astype(F32) * inv
        scaled = normed_grad[:, here] * gain[:, here]
        out_ref[:, here] = (res[:, here].astype(F32) + inv * (scaled - unit * inner)).astype(BF16)

    for copy in g_1:
        copy.wait_recv()
    g2[y] = jnp.sum(g1[...], axis=0)
    g_2 = [
        go(remote(g2.at[y], g2.at[y], g2_s.at[dy - 1], g2_r.at[dy - 1], device(dy=dy))) for dy in range(1, NY)
    ]
    for copy in g_2:
        copy.wait_recv()
    g3[z] = jnp.sum(g2[...], axis=0)
    g_3 = [
        go(remote(g3.at[z], g3.at[z], g3_s.at[dz - 1], g3_r.at[dz - 1], device(zz=(z + dz) % nz)))
        for dz in range(1, nz)
    ]

    for copy in z_all:
        copy.wait_recv()
    total = own_sum[aligned(zl, block), 0 : 2 * cols]
    for i in range(nz - 1):
        total = total + z_recv[i].astype(F32)
    total = total * scale
    kw_ref[...] = total[:, :cols]
    vw_ref[...] = total[:, cols:]

    for copy in g_3:
        copy.wait_recv()
    gf[me] = jnp.sum(g3[...], axis=0) * scale
    g_4 = [
        go(remote(gf.at[me], gf.at[me], g4_s.at[i], g4_r.at[i], device(dc=dc, dx=dx))) for i, (dx, dc) in enumerate(xc)
    ]
    for copy in g_4:
        copy.wait_recv()
    gain_out[...] = gf[...]
    for copy in sends:
        copy.wait_send()


def per_device(hidden_in, norm_gain, resid_grad, key_grad, value_grad, key_matrix, value_matrix):
    scale = 1.0 / math.sqrt(key_grad.shape[0] * lax.axis_size("dp"))
    rows, width = hidden_in.shape
    cols = key_matrix.shape[1]
    half = rows * NX
    block = width // (NC * NY * NZL)
    shard = width // NC // NY
    nz = NZL * NZH
    part = width // (NX * NC)
    dma = pltpu.SemaphoreType.DMA
    loose = pl.BlockSpec(memory_space=pltpu.HBM)
    vmem = pl.BlockSpec(memory_space=pltpu.VMEM)
    input_grad, key_sum, value_sum, gain_sum = pl.pallas_call(
        functools.partial(kernel, scale),
        out_shape=(
            jax.ShapeDtypeStruct((rows, width), BF16),
            jax.ShapeDtypeStruct((block, cols), F32),
            jax.ShapeDtypeStruct((block, cols), F32),
            jax.ShapeDtypeStruct((NX * NC, 1, part), F32),
        ),
        in_specs=[loose] * 7,
        out_specs=(vmem, vmem, vmem, vmem),
        scratch_shapes=[
            pltpu.VMEM((rows, width), BF16),
            pltpu.VMEM((rows, width), BF16),
            pltpu.VMEM((1, width), F32),
            pltpu.VMEM((rows, 1), F32),
            pltpu.VMEM((rows, width), BF16),
            pltpu.VMEM((NC, NY, shard, rows), BF16),
            pltpu.VMEM((NC, NY, shard, half), BF16),
            pltpu.VMEM((NC, NZH * 2 * cols, half), BF16),
            pltpu.VMEM((2 * cols, half), BF16),
            pltpu.VMEM((NZH * NX, 2 * cols, rows), BF16),
            pltpu.VMEM((NZH * NX, 2 * cols, width), BF16),
            pltpu.VMEM((rows, width), F32),
            pltpu.VMEM((NY - 1, shard, NZH * 2 * cols), BF16),
            pltpu.VMEM((NY - 1, shard, NZH * 2 * cols), BF16),
            pltpu.VMEM((shard, NZH * 2 * cols), F32),
            pltpu.VMEM((NZH, shard, 2 * cols), BF16),
            pltpu.VMEM((nz - 1, block, 2 * cols), BF16),
            pltpu.VMEM((NX * NC, 1, part), F32),
            pltpu.VMEM((NX * NC, 1, part), F32),
            pltpu.VMEM((NY, 1, part), F32),
            pltpu.VMEM((nz, 1, part), F32),
            pltpu.VMEM((NX * NC, 1, part), F32),
            dma((10,)),
            dma,
            dma,
            dma((2 * (NX - 1),)),
            dma((2 * (NX - 1),)),
            dma((2 * NY,)),
            dma((2 * NY,)),
            dma,
            dma,
            dma,
            dma,
            dma((2,)),
            dma((2,)),
            dma((2 * NX,)),
            dma((2 * NX,)),
            dma((NX * NC - 1,)),
            dma((NX * NC - 1,)),
            dma((NY - 1,)),
            dma((NY - 1,)),
            dma((nz - 1,)),
            dma((nz - 1,)),
            dma((NX * NC - 1,)),
            dma((NX * NC - 1,)),
            dma((NY - 1,)),
            dma((NY - 1,)),
            dma((nz - 1,)),
            dma((nz - 1,)),
            dma((NX * NC - 1,)),
            dma((NX * NC - 1,)),
        ],
        compiler_params=pltpu.CompilerParams(collective_id=0, has_side_effects=True, vmem_limit_bytes=62 * 1024 * 1024),
    )(
        hidden_in,
        norm_gain.reshape(1, width),
        resid_grad,
        key_grad.T,
        value_grad.T,
        key_matrix.T,
        value_matrix.T,
    )
    return input_grad, key_sum, value_sum, gain_sum.reshape(width)


def solution(mesh):
    return jax.shard_map(
        per_device,
        mesh=mesh,
        in_specs=(
            P(("dp", "seq"), None),
            P(),
            P(("dp", "seq"), None),
            P("dp", "seq"),
            P("dp", "seq"),
            P(None, "seq"),
            P(None, "seq"),
        ),
        out_specs=(P(("dp", "seq"), None), P("dp", "seq"), P("dp", "seq"), P()),
        check_vma=False,
    )
```

time: 1300 us -> 93.2 us (0.07)
  waiting for transfers between devices: 1130 us -> 0 us
  blocking collectives: 101 us -> 0 us
  Pallas kernels: 0 us -> 88.4 us
  starting transfers between devices: 21.7 us -> 0 us
  matrix products: 14.1 us -> 0 us
  between operations: 13.9 us -> 0.65 us
    reduce_scatter x2 -> x0, waiting for transfers between devices: 741 us -> none  [the longest x1 430 us: per_device(): lax.psum_scatter(key_next, 'dp', scatter_dimension=0, tiled=True)]
    all_gather x3 -> x0, waiting for transfers between devices: 376 us -> none  [the longest x1 174 us: per_device(): normed_piece = lax.all_gather(normed, 'seq', axis=0, tiled=True)]
    psum x1 -> x0, blocking collectives: 101 us -> none  [per_device(): lax.psum(jnp.sum(normed_grad * unit_rows, axis=0), ('dp', 'seq'))]
    pallas_call x0 -> x1, Pallas kernels: none -> 88.4 us  [per_device(): pl.pallas_call(functools.partial(kernel, scale), out_shape=(jax.ShapeDtyp...]
    all_to_all x2 -> x0, starting transfers between devices: 21.5 us -> none  [the longest x1 18.1 us: per_device(): lax.all_to_all(key_output_gradient, 'seq', split_axis=0, concat_axis=1, t...]
    dot_general x4 -> x0, matrix products: 14.1 us -> none  [the longest x1 4.49 us: per_device(): jnp.einsum('td,tc->dc', normed_piece, key_output_gradient, preferred_elem...]
  transfers between devices with their start and end apart: 7 -> 0, of which waited for: 6 -> 0; matrix products, arithmetic and copies ran while one was open for 1% -> 0% of each run, Pallas kernels for 0% -> 0%
where the time goes in v1:
time: 93.2 us; the launch traced here: 93 us
  Pallas kernels  88.4 us (95%)
  local copies, waits for them, and re-layouts  3.92 us (4%)
    pallas_call x1, Pallas kernels, per_device(): pl.pallas_call(functools.partial(kernel, scale), out_shape=(jax.ShapeDtyp...  88.4 us
    unnamed x10, local copies, waits for them, and re-layouts  3.92 us

profile of v1, /device:TPU:1, one launch (start us, length us, event | category | flops | bytes accessed | tf_op | source)
XLA Modules:
  0.0 93.0 jit_solution(8591482197089575923)
XLA Ops:
  0.6 88.4 %shard_map.102 = (bf16[128,2048]{1,0:T(8,128)(2,1)}, f32[32,64]{1,0:T(8,128)}, f32[32,64]{1,0:T(8,128)}, f32[8,1,256]{2,1,0:T(1,128)}) custom-call(bf16[128,2048]{1,0:T(8,128)(2,1)} %hid_hbm.1, f32[1,2048]{1,0:T(1,128)} %bitcast.10, bf16[128,2048]{1,0:T(8,128)(2,1)} %res_hbm.1, bf16[64,1024]{1,0:T(8,128)(2,1)} %bitcast.8, bf16[64,1024]{1,0:T(8,128)(2,1)} %bitcast.9, ...), custom_call_target="tpu_custom_call" | custom-call | tf_op jit(solution)/shard_map/pallas_call | solution.py:366
  89.0 0.0 copy-start.1
  89.0 1.9 %copy.15 = bf16[128,2048]{1,0:T(8,128)(2,1)} copy(bf16[128,2048]{1,0:T(8,128)(2,1)} %get-tuple-element.16) | data formatting | bytes 1048576
  90.9 0.0 copy-done.1
  90.9 0.0 copy-start
  90.9 0.6 copy.16
  91.5 0.1 copy-done
  91.6 0.0 copy-start.2
  91.7 0.6 copy.17
  92.3 0.1 copy-done.2
  92.4 0.6 copy.18
Async XLA Ops:
  89.0 1.9 %copy-start.1 = (f32[32,64]{1,0:T(8,128)S(1)}, f32[32,64]{1,0:T(8,128)}, u32[]{:S(2)}) copy-start(f32[32,64]{1,0:T(8,128)} %get-tuple-element.17) | copy-start | bytes 24580
  90.9 0.7 copy-start
  91.6 0.7 copy-start.2

commit v2 on v1

--- a/solution.py
+++ b/solution.py
@@ -12,6 +12,7 @@
 MESH = pl.DeviceIdType.MESH
 BF16, F32 = jnp.bfloat16, jnp.float32
 NX, NY, NZL, NZH, NC = 4, 4, 8, 2, 2
+SPLIT = 4
 NT_DIMS = (((1,), (1,)), ((), ()))
 
 
@@ -30,6 +31,7 @@
     gain_out,
     hid,
     res,
+    out_buf,
     gain,
     inv_ref,
     nrm,
@@ -45,9 +47,9 @@
     own_sum,
     z_send,
     z_recv,
-    ga,
-    g1,
-    g2,
+    wt,
+    wt_far,
+    gx,
     g3,
     gf,
     load_sem,
@@ -71,10 +73,10 @@
     y_r,
     z_s,
     z_r,
-    g1_s,
-    g1_r,
-    g2_s,
-    g2_r,
+    wt_s,
+    wt_r,
+    gx_s,
+    gx_r,
     g3_s,
     g3_r,
     g4_s,
@@ -121,7 +123,8 @@
     barrier = pltpu.get_barrier_semaphore()
     xc = [(dx, dc) for dx in range(NX) for dc in range(NC) if dx or dc]
     peers = [device(dc=dc, dx=dx) for dx, dc in xc]
-    peers += [device(dy=dy) for dy in range(1, NY)]
+    yc = [(dy, dc) for dy in range(NY) for dc in range(NC) if dy or dc]
+    peers += [device(dc=dc, dy=dy) for dy, dc in yc if dy]
     peers += [device(zz=(z + dz) % nz) for dz in range(1, nz)]
     for peer in peers:
         pl.semaphore_signal(barrier, inc=1, device_id=peer, device_id_type=MESH)
@@ -144,6 +147,12 @@
             nt[bc, by, bz * block : (bz + 1) * block] = turned[part * block : (part + 1) * block]
     for load in loads[2:8]:
         load.wait()
+    for at in range(0, width, lane):
+        turned = w_all[0, :, at : at + lane].T
+        for part in range(lane // block):
+            b = at // block + part
+            bc, by, bz = b % NC, (b // NC) % NY, b // (NC * NY)
+            wt[bc, by, bz * block : (bz + 1) * block] = turned[part * block : (part + 1) * block]
     pl.semaphore_wait(barrier, len(peers))
 
     q = aligned(c * NY + y, piece)
@@ -154,12 +163,52 @@
         sends.append(copy)
         return copy
 
-    w_z = go(remote(w_all.at[0, :, q], w_all.at[NX, :, q], wz_s, wz_r, device(zz=nz - 1 - z)))
+    around = [(1, 0), (NX - 1, 1)]
+    sides = [(1, 0), (NY - 1, 1)]
+
+    share = NZL // 2
+    deep = 2 * cols // share
+    w_q = go(
+        remote(
+            w_all.at[0, aligned(share - 1 - zl % share, deep), q],
+            w_all.at[NX, aligned(share - 1 - zl % share, deep), q],
+            wz_s.at[0],
+            wz_r.at[0],
+            device(zz=nz - 1 - z),
+        )
+    )
+
+    tall = piece // share
+
+    def turned_send():
+        rows_at = aligned(share - 1 - zl % share, tall)
+        return go(remote(wt.at[c, y, rows_at], wt_far.at[rows_at], wt_s.at[0], wt_r.at[0], device(zz=nz - 1 - z)))
+
+    def turned_share():
+        wt_q.wait_recv()
+        ref = wt_far.at[aligned(zl % share, tall)]
+        return [
+            go(remote(ref, ref, wt_s.at[d], wt_r.at[d], device(zz=z - zl % share + (zl + d) % share)))
+            for d in range(1, share)
+        ]
+
+    def x_sends(rel):
+        return [
+            go(
+                remote(
+                    w_all.at[rel * NX, :, q],
+                    w_all.at[rel * NX + dx, :, q],
+                    wx_s.at[rel * NX + dx],
+                    wx_r.at[rel * NX + dx],
+                    device(dx=dx),
+                )
+            )
+            for dx in range(1, NX)
+        ]
+
+    w_x = x_sends(0)
     k_z = go(remote(kv_far, kv.at[0, pl.ds(2 * cols, 2 * cols)], kz_s, kz_r, device(zz=(z + nz // 2) % nz)))
-    w_x = [
-        go(remote(w_all.at[0, :, q], w_all.at[dx, :, q], wx_s.at[dx - 1], wx_r.at[dx - 1], device(dx=dx)))
-        for dx in range(1, NX)
-    ]
+    wt_q = turned_send()
     k_c = go(remote(kv.at[0, pl.ds(0, 2 * cols)], kv.at[1, pl.ds(0, 2 * cols)], kc_s.at[0], kc_r.at[0], device(dc=1)))
 
     def token_sends(rel):
@@ -176,49 +225,95 @@
             for dx in range(1, NX)
         ]
 
-    k_x = token_sends(0)
     mine = aligned(x, rows)
-    n_all = []
-    for i, (dx, dc) in enumerate(xc):
-        n_all.append(
-            go(remote(nt.at[(c + dc) % NC], ng_all.at[dc, :, :, mine], n_s.at[i], n_r.at[i], device(dc=dc, dx=dx)))
-        )
-    own = pltpu.make_async_copy(nt.at[c], ng_all.at[0, :, :, mine], load_sem.at[9])
-    own.start()
-
-    def y_sends(first, count, rel):
+
+    order = [d for d in (2, 1, 3, 0) if d < NY]
+
+    def normed_sends(i):
+        to = (y + order[i]) % NY
         return [
             go(
                 remote(
-                    w_all.at[pl.ds(first, count), :, q],
-                    w_all.at[pl.ds(first, count), :, q],
-                    wy_s.at[rel * NY + dy],
-                    wy_r.at[rel * NY + dy],
-                    device(dy=dy),
+                    nt.at[(c + dc) % NC, to],
+                    ng_all.at[dc, to, :, mine],
+                    n_s.at[(i * 2 + way) * NC + dc],
+                    n_r.at[(i * 2 + way) * NC + dc],
+                    device(dc=dc, dx=dx),
                 )
             )
-            for dy in range(1, NY)
+            for way, (dx, part) in enumerate(around)
+            for dc in range(NC)
         ]
 
+    def normed_pass(i):
+        to = (y + order[i]) % NY
+        deep = ng_all.shape[2] // 2
+        out = []
+        for way, (dx, part) in enumerate(around):
+            for dc in range(NC):
+                n_direct[i][way * NC + dc].wait_recv()
+                ref = ng_all.at[dc, to, pl.ds(part * deep, deep), aligned((x - dx + NX) % NX, rows)]
+                at = ((NY + i) * 2 + way) * NC + dc
+                out.append(go(remote(ref, ref, n_s.at[at], n_r.at[at], device(dx=dx))))
+        return out
+
+    n_direct = [normed_sends(0)]
+    n_core = go(remote(nt.at[(c + 1) % NC], ng_all.at[1, :, :, mine], n_s.at[4 * NY * NC], n_r.at[4 * NY * NC], device(dc=1)))
+    own = pltpu.make_async_copy(nt.at[c], ng_all.at[0, :, :, mine], load_sem.at[9])
+    own.start()
+    k_x = token_sends(0)
+    n_direct.append(normed_sends(1))
+
+    def y_sends(rel):
+        slots = pl.ds(rel * NX + (0 if rel else 1), NX if rel else NX - 1)
+        first, second = [], []
+        for turn, into in ((0, first), (1, second)):
+            for way, (dy, part) in enumerate(sides):
+                lanes = half_piece(c * NY + y, part if turn == 0 else 1 - part)
+                at = rel * 6 + way * 2 + turn
+                ref = w_all.at[slots, :, lanes]
+                into.append(go(remote(ref, ref, wy_s.at[at], wy_r.at[at], device(dy=dy))))
+        return first, second
+
+    def half_piece(index, part):
+        return pl.ds(pl.multiple_of(index * piece + part * (piece // 2), piece // 2), piece // 2)
+
+    def y_pass(rel, first):
+        slots = pl.ds(rel * NX + (0 if rel else 1), NX if rel else NX - 1)
+        out = []
+        for way, (dy, part) in enumerate(sides):
+            first[way].wait_recv()
+            lanes = half_piece(c * NY + (y - dy + NY) % NY, part)
+            at = rel * 6 + 4 + way
+            ref = w_all.at[slots, :, lanes]
+            out.append(go(remote(ref, ref, wy_s.at[at], wy_r.at[at], device(dy=dy))))
+        return out
+
     for copy in w_x:
         copy.wait_recv()
-    w_y = y_sends(1, NX - 1, 0)
-    w_z.wait_recv()
-    w_x2 = [
-        go(
-            remote(
-                w_all.at[NX, :, q],
-                w_all.at[NX + dx, :, q],
-                wx_s.at[NX - 1 + dx - 1],
-                wx_r.at[NX - 1 + dx - 1],
-                device(dx=dx),
-            )
-        )
-        for dx in range(1, NX)
+    w_y1, w_y2 = y_sends(0)
+    w_q.wait_recv()
+    ref = w_all.at[NX, aligned(zl % share, deep), q]
+    w_z = [
+        go(remote(ref, ref, wz_s.at[d], wz_r.at[d], device(zz=z - zl % share + (zl + d) % share)))
+        for d in range(1, share)
     ]
+    n_pass = [normed_pass(0)]
+    for copy in w_z:
+        copy.wait_recv()
+    w_x2 = x_sends(1)
+    n_direct.append(normed_sends(2))
+    w_y3 = y_pass(0, w_y1)
+    n_pass.append(normed_pass(1))
+    n_direct.append(normed_sends(3))
     for copy in w_x2:
         copy.wait_recv()
-    w_y2 = y_sends(NX, NX, 1)
+    w_y4, w_y5 = y_sends(1)
+    for copy in w_y2 + w_y3:
+        copy.wait_recv()
+    side = aligned(c, width // NC)
+    ref = w_all.at[pl.ds(1, NX - 1), :, side]
+    w_c = [go(remote(ref, ref, wc_s.at[0], wc_r.at[0], device(dc=1)))]
 
     k_z.wait_recv()
     k_c2 = go(
@@ -231,15 +326,14 @@
         )
     )
     k_x += token_sends(1)
-    own.wait()
-    for copy in n_all:
-        copy.wait_recv()
-    k_c.wait_recv()
-    k_c2.wait_recv()
 
     y_all = []
-    for dy in [d for d in (2, 1, 3, 0) if d < NY]:
+
+    def weight_chunk(i):
+        dy = order[i]
         to = (y + dy) % NY
+        for copy in n_pass[i]:
+            copy.wait_recv()
         total = lax.dot_general(ng_all[0, to], kv[0], NT_DIMS, preferred_element_type=F32)
         total = total + lax.dot_general(ng_all[1, to], kv[1], NT_DIMS, preferred_element_type=F32)
         if dy:
@@ -248,13 +342,21 @@
         else:
             own_sum[...] = total
 
-    side = aligned(c, width // NC)
-    for copy in w_y + w_y2:
-        copy.wait_recv()
-    w_c = go(
-        remote(w_all.at[pl.ds(1, 2 * NX - 1), :, side], w_all.at[pl.ds(1, 2 * NX - 1), :, side], wc_s, wc_r, device(dc=1))
-    )
-
+    own.wait()
+    for copy in [n_core, k_c, k_c2]:
+        copy.wait_recv()
+    w_t = turned_share()
+    weight_chunk(0)
+    n_pass.append(normed_pass(2))
+    w_y6 = y_pass(1, w_y4)
+    weight_chunk(1)
+    n_pass.append(normed_pass(3))
+    weight_chunk(2)
+    weight_chunk(3)
+    for copy in w_y5 + w_y6:
+        copy.wait_recv()
+    ref = w_all.at[pl.ds(NX, NX), :, side]
+    w_c.append(go(remote(ref, ref, wc_s.at[1], wc_r.at[1], device(dc=1))))
     for copy in y_all:
         copy.wait_recv()
     total = own_sum[...]
@@ -278,57 +380,51 @@
             )
         )
 
+    for copy in w_t:
+        copy.wait_recv()
+    deepest = 2 * cols
+    both = own_sum[:, :deepest] * wt[c, y].astype(F32) + own_sum[:, deepest:] * wt_far[...].astype(F32)
+    gx[x] = jnp.sum(both.T, axis=0, keepdims=True)
+    g_1 = [go(remote(gx.at[x], gx.at[x], gx_s.at[dx - 1], gx_r.at[dx - 1], device(dx=dx))) for dx in range(1, NX)]
+    for copy in g_1:
+        copy.wait_recv()
+    g3[z] = jnp.sum(gx[...], axis=0)
+    g_3 = [
+        go(remote(g3.at[z], g3.at[z], g3_s.at[dz - 1], g3_r.at[dz - 1], device(zz=(z + dz) % nz)))
+        for dz in range(1, nz)
+    ]
     for copy in k_x:
         copy.wait_recv()
     for rel in range(NZH):
         kv_tok[rel * NX] = kv[0, rel * 2 * cols : (rel + 1) * 2 * cols, mine]
-    w_c.wait_recv()
     tok = kv_tok[...].reshape(-1, rows).T
     inner = jnp.zeros((rows, 1), F32)
     inv = inv_ref[...]
-    chunk = min(256, width)
-    for at in range(0, width, chunk):
-        here = slice(at, at + chunk)
-        weights = w_all[:, :, here].reshape(-1, chunk)
-        grad = jnp.dot(tok, weights, preferred_element_type=F32)
-        unit = hid[:, here].astype(F32) * inv
-        normed_grad[:, here] = grad
-        both = grad * unit
-        inner = inner + jnp.sum(both * gain[:, here], axis=-1, keepdims=True)
-        total = jnp.sum(both, axis=0, keepdims=True)
-        part = width // (NX * NC)
-        for i in range(chunk // part):
-            ga[at // part + i] = total[:, i * part : (i + 1) * part]
+    chunk = min(256, width // NC)
+    for dc in range(NC):
+        if dc:
+            for copy in w_c:
+                copy.wait_recv()
+        for i in range(width // NC // chunk):
+            at = ((c + dc) % NC) * (width // NC // chunk) + i
+            here = aligned(at, chunk)
+            weights = w_all[:, :, here].reshape(-1, chunk)
+            grad = jnp.dot(tok, weights, preferred_element_type=F32)
+            unit = hid[:, here].astype(F32) * inv
+            normed_grad[:, here] = grad
+            both = grad * unit
+            inner = inner + jnp.sum(both * gain[:, here], axis=-1, keepdims=True)
     inner = inner * (1.0 / width)
-
-    g_1 = []
-    me = x * NC + c
-    for i, (dx, dc) in enumerate(xc):
-        to = ((x + dx) % NX) * NC + (c + dc) % NC
-        g_1.append(go(remote(ga.at[to], g1.at[me], g1_s.at[i], g1_r.at[i], device(dc=dc, dx=dx))))
-    g1[me] = ga[me]
 
     loads[8].wait()
     for at in range(0, width, chunk):
         here = slice(at, at + chunk)
         unit = hid[:, here].astype(F32) * inv
         scaled = normed_grad[:, here] * gain[:, here]
-        out_ref[:, here] = (res[:, here].astype(F32) + inv * (scaled - unit * inner)).astype(BF16)
-
-    for copy in g_1:
-        copy.wait_recv()
-    g2[y] = jnp.sum(g1[...], axis=0)
-    g_2 = [
-        go(remote(g2.at[y], g2.at[y], g2_s.at[dy - 1], g2_r.at[dy - 1], device(dy=dy))) for dy in range(1, NY)
-    ]
-    for copy in g_2:
-        copy.wait_recv()
-    g3[z] = jnp.sum(g2[...], axis=0)
-    g_3 = [
-        go(remote(g3.at[z], g3.at[z], g3_s.at[dz - 1], g3_r.at[dz - 1], device(zz=(z + dz) % nz)))
-        for dz in range(1, nz)
-    ]
-
+        out_buf[:, here] = (res[:, here].astype(F32) + inv * (scaled - unit * inner)).astype(BF16)
+    stores = [pltpu.make_async_copy(out_buf, out_ref, load_sem.at[10])]
+    for store in stores:
+        store.start()
     for copy in z_all:
         copy.wait_recv()
     total = own_sum[aligned(zl, block), 0 : 2 * cols]
@@ -340,15 +436,40 @@
 
     for copy in g_3:
         copy.wait_recv()
-    gf[me] = jnp.sum(g3[...], axis=0) * scale
+    me = y * NC + c
+    gf[me] = jnp.sum(g3[...], axis=0)
     g_4 = [
-        go(remote(gf.at[me], gf.at[me], g4_s.at[i], g4_r.at[i], device(dc=dc, dx=dx))) for i, (dx, dc) in enumerate(xc)
+        go(remote(gf.at[me], gf.at[me], g4_s.at[i], g4_r.at[i], device(dc=dc, dy=dy))) for i, (dy, dc) in enumerate(yc)
     ]
     for copy in g_4:
         copy.wait_recv()
-    gain_out[...] = gf[...]
+    for p in range(NY * NC):
+        for b in range(NZL):
+            at = (b * NY * NC + p) * block
+            there = slice(at, at + block)
+            gain_out[:, there] = gf[p][:, b * block : (b + 1) * block] / gain[:, there] * scale
+    for store in stores:
+        store.wait()
     for copy in sends:
         copy.wait_send()
+
+
+def hand_over(grad, key, value, gain, grad_out, key_out, value_out, gain_out, held, in_sem, out_sem):
+    deep = grad.shape[0] // SPLIT
+    ins, outs = [], []
+    for i in range(SPLIT):
+        rows = pl.ds(i * deep, deep)
+        ins.append(pltpu.make_async_copy(grad.at[rows], held.at[rows], in_sem.at[i]))
+        outs.append(pltpu.make_async_copy(held.at[rows], grad_out.at[rows], out_sem.at[i]))
+    for copy in ins:
+        copy.start()
+    for src, dst in ((key, key_out), (value, value_out), (gain, gain_out)):
+        dst[...] = src[...]
+    for first, second in zip(ins, outs):
+        first.wait()
+        second.start()
+    for copy in outs:
+        copy.wait()
 
 
 def per_device(hidden_in, norm_gain, resid_grad, key_grad, value_grad, key_matrix, value_matrix):
@@ -359,7 +480,6 @@
     block = width // (NC * NY * NZL)
     shard = width // NC // NY
     nz = NZL * NZH
-    part = width // (NX * NC)
     dma = pltpu.SemaphoreType.DMA
     loose = pl.BlockSpec(memory_space=pltpu.HBM)
     vmem = pl.BlockSpec(memory_space=pltpu.VMEM)
@@ -369,11 +489,12 @@
             jax.ShapeDtypeStruct((rows, width), BF16),
             jax.ShapeDtypeStruct((block, cols), F32),
             jax.ShapeDtypeStruct((block, cols), F32),
-            jax.ShapeDtypeStruct((NX * NC, 1, part), F32),
+            jax.ShapeDtypeStruct((1, width), F32),
         ),
         in_specs=[loose] * 7,
-        out_specs=(vmem, vmem, vmem, vmem),
+        out_specs=(loose, vmem, vmem, vmem),
         scratch_shapes=[
+            pltpu.VMEM((rows, width), BF16),
             pltpu.VMEM((rows, width), BF16),
             pltpu.VMEM((rows, width), BF16),
             pltpu.VMEM((1, width), F32),
@@ -391,40 +512,40 @@
             pltpu.VMEM((shard, NZH * 2 * cols), F32),
             pltpu.VMEM((NZH, shard, 2 * cols), BF16),
             pltpu.VMEM((nz - 1, block, 2 * cols), BF16),
-            pltpu.VMEM((NX * NC, 1, part), F32),
-            pltpu.VMEM((NX * NC, 1, part), F32),
-            pltpu.VMEM((NY, 1, part), F32),
-            pltpu.VMEM((nz, 1, part), F32),
-            pltpu.VMEM((NX * NC, 1, part), F32),
-            dma((10,)),
-            dma,
-            dma,
-            dma((2 * (NX - 1),)),
-            dma((2 * (NX - 1),)),
-            dma((2 * NY,)),
-            dma((2 * NY,)),
-            dma,
-            dma,
+            pltpu.VMEM((NC, NY, shard, 2 * cols), BF16),
+            pltpu.VMEM((shard, 2 * cols), BF16),
+            pltpu.VMEM((NX, 1, shard), F32),
+            pltpu.VMEM((nz, 1, shard), F32),
+            pltpu.VMEM((NY * NC, 1, shard), F32),
+            dma((11,)),
+            dma((NZL // 2,)),
+            dma((NZL // 2,)),
+            dma((2 * NX,)),
+            dma((2 * NX,)),
+            dma((12,)),
+            dma((12,)),
+            dma((2,)),
+            dma((2,)),
             dma,
             dma,
             dma((2,)),
             dma((2,)),
             dma((2 * NX,)),
             dma((2 * NX,)),
-            dma((NX * NC - 1,)),
-            dma((NX * NC - 1,)),
+            dma((4 * NY * NC + 1,)),
+            dma((4 * NY * NC + 1,)),
             dma((NY - 1,)),
             dma((NY - 1,)),
             dma((nz - 1,)),
             dma((nz - 1,)),
-            dma((NX * NC - 1,)),
-            dma((NX * NC - 1,)),
-            dma((NY - 1,)),
-            dma((NY - 1,)),
+            dma((NZL // 2,)),
+            dma((NZL // 2,)),
+            dma((NX - 1,)),
+            dma((NX - 1,)),
             dma((nz - 1,)),
             dma((nz - 1,)),
-            dma((NX * NC - 1,)),
-            dma((NX * NC - 1,)),
+            dma((NY * NC - 1,)),
+            dma((NY * NC - 1,)),
         ],
         compiler_params=pltpu.CompilerParams(collective_id=0, has_side_effects=True, vmem_limit_bytes=62 * 1024 * 1024),
     )(
@@ -436,6 +557,14 @@
         key_matrix.T,
         value_matrix.T,
     )
+    done = (input_grad, key_sum, value_sum, gain_sum)
+    input_grad, key_sum, value_sum, gain_sum = pl.pallas_call(
+        hand_over,
+        out_shape=tuple(jax.ShapeDtypeStruct(a.shape, a.dtype) for a in done),
+        in_specs=[loose] + [vmem] * 3,
+        out_specs=(loose,) + (vmem,) * 3,
+        scratch_shapes=[pltpu.VMEM((rows, width), BF16), dma((SPLIT,)), dma((SPLIT,))],
+    )(*done)
     return input_grad, key_sum, value_sum, gain_sum.reshape(width)
 
 

time: 93.2 us -> 76.8 us (0.82)
  Pallas kernels: 88.4 us -> 76 us
  local copies, waits for them, and re-layouts: 3.92 us -> 0 us
    pallas_call x1, Pallas kernels: 88.4 us -> 72.8 us  [per_device(): pl.pallas_call(functools.partial(kernel, scale), out_shape=(jax.ShapeDtyp...]
    unnamed x10 -> x0, local copies, waits for them, and re-layouts: 3.92 us -> none
    pallas_call x0 -> x1, Pallas kernels: none -> 3.17 us  [per_device(): pl.pallas_call(hand_over, out_shape=tuple((jax.ShapeDtypeStruct(a.shape,...]
where the time goes in v2:
time: 76.8 us; the launch traced here: 76.6 us
  Pallas kernels  76 us (99%)
    pallas_call x1, Pallas kernels, per_device(): pl.pallas_call(functools.partial(kernel, scale), out_shape=(jax.ShapeDtyp...  72.8 us
    pallas_call x1, Pallas kernels, per_device(): pl.pallas_call(hand_over, out_shape=tuple((jax.ShapeDtypeStruct(a.shape,...  3.17 us

profile of v2, /device:TPU:1, one launch (start us, length us, event | category | flops | bytes accessed | tf_op | source)
XLA Modules:
  0.0 76.6 jit_solution(9963639567900770688)
XLA Ops:
  0.6 72.8 %shard_map.102 = (bf16[128,2048]{1,0:T(8,128)(2,1)}, f32[32,64]{1,0:T(8,128)}, f32[32,64]{1,0:T(8,128)}, f32[1,2048]{1,0:T(1,128)}) custom-call(bf16[128,2048]{1,0:T(8,128)(2,1)} %hid_hbm.1, f32[1,2048]{1,0:T(1,128)} %bitcast.10, bf16[128,2048]{1,0:T(8,128)(2,1)} %res_hbm.1, bf16[64,1024]{1,0:T(8,128)(2,1)} %bitcast.8, bf16[64,1024]{1,0:T(8,128)(2,1)} %bitcast.9, ...), custom_call_target="tpu_custom_call" | custom-call | tf_op jit(solution)/shard_map/pallas_call | solution.py:486
  73.4 3.2 %shard_map.103 = (bf16[128,2048]{1,0:T(8,128)(2,1)}, f32[32,64]{1,0:T(8,128)}, f32[32,64]{1,0:T(8,128)}, f32[1,2048]{1,0:T(1,128)}) custom-call(bf16[128,2048]{1,0:T(8,128)(2,1)} %get-tuple-element.12.grad, f32[32,64]{1,0:T(8,128)} %get-tuple-element.13.key, f32[32,64]{1,0:T(8,128)} %get-tuple-element.14.value, f32[1,2048]{1,0:T(1,128)} %get-tuple-element.15.gain), custom_call_target="tpu_custom_call" | custom-call | tf_op jit(solution)/shard_map/pallas_call | solution.py:561

commit v3 on v2

--- a/solution.py
+++ b/solution.py
@@ -299,16 +299,13 @@
         for d in range(1, share)
     ]
     n_pass = [normed_pass(0)]
-    for copy in w_z:
-        copy.wait_recv()
-    w_x2 = x_sends(1)
     n_direct.append(normed_sends(2))
     w_y3 = y_pass(0, w_y1)
     n_pass.append(normed_pass(1))
     n_direct.append(normed_sends(3))
-    for copy in w_x2:
-        copy.wait_recv()
-    w_y4, w_y5 = y_sends(1)
+    for copy in w_z:
+        copy.wait_recv()
+    w_x2 = x_sends(1)
     for copy in w_y2 + w_y3:
         copy.wait_recv()
     side = aligned(c, width // NC)
@@ -348,15 +345,13 @@
     w_t = turned_share()
     weight_chunk(0)
     n_pass.append(normed_pass(2))
-    w_y6 = y_pass(1, w_y4)
     weight_chunk(1)
     n_pass.append(normed_pass(3))
     weight_chunk(2)
+    for copy in w_x2:
+        copy.wait_recv()
+    w_y4, w_y5 = y_sends(1)
     weight_chunk(3)
-    for copy in w_y5 + w_y6:
-        copy.wait_recv()
-    ref = w_all.at[pl.ds(NX, NX), :, side]
-    w_c.append(go(remote(ref, ref, wc_s.at[1], wc_r.at[1], device(dc=1))))
     for copy in y_all:
         copy.wait_recv()
     total = own_sum[...]
@@ -393,6 +388,11 @@
         go(remote(g3.at[z], g3.at[z], g3_s.at[dz - 1], g3_r.at[dz - 1], device(zz=(z + dz) % nz)))
         for dz in range(1, nz)
     ]
+    w_y6 = y_pass(1, w_y4)
+    for copy in w_y5 + w_y6:
+        copy.wait_recv()
+    ref = w_all.at[pl.ds(NX, NX), :, side]
+    w_c.append(go(remote(ref, ref, wc_s.at[1], wc_r.at[1], device(dc=1))))
     for copy in k_x:
         copy.wait_recv()
     for rel in range(NZH):
@@ -443,18 +443,14 @@
     ]
     for copy in g_4:
         copy.wait_recv()
-    for p in range(NY * NC):
-        for b in range(NZL):
-            at = (b * NY * NC + p) * block
-            there = slice(at, at + block)
-            gain_out[:, there] = gf[p][:, b * block : (b + 1) * block] / gain[:, there] * scale
+    gain_out[...] = gf[...]
     for store in stores:
         store.wait()
     for copy in sends:
         copy.wait_send()
 
 
-def hand_over(grad, key, value, gain, grad_out, key_out, value_out, gain_out, held, in_sem, out_sem):
+def hand_over(scale, grad, key, value, gain, norm_gain, grad_out, key_out, value_out, gain_out, held, in_sem, out_sem):
     deep = grad.shape[0] // SPLIT
     ins, outs = [], []
     for i in range(SPLIT):
@@ -463,11 +459,17 @@
         outs.append(pltpu.make_async_copy(held.at[rows], grad_out.at[rows], out_sem.at[i]))
     for copy in ins:
         copy.start()
-    for src, dst in ((key, key_out), (value, value_out), (gain, gain_out)):
-        dst[...] = src[...]
+    key_out[...] = key[...]
+    value_out[...] = value[...]
+    parts, block = gain.shape[0], gain.shape[2] // NZL
+    for p in range(parts):
+        for b in range(NZL):
+            at = (b * parts + p) * block
+            gain_out[:, at : at + block] = gain[p][:, b * block : (b + 1) * block] * scale
     for first, second in zip(ins, outs):
         first.wait()
         second.start()
+    gain_out[...] = gain_out[...] / norm_gain[...]
     for copy in outs:
         copy.wait()
 
@@ -489,7 +491,7 @@
             jax.ShapeDtypeStruct((rows, width), BF16),
             jax.ShapeDtypeStruct((block, cols), F32),
             jax.ShapeDtypeStruct((block, cols), F32),
-            jax.ShapeDtypeStruct((1, width), F32),
+            jax.ShapeDtypeStruct((NY * NC, 1, shard), F32),
         ),
         in_specs=[loose] * 7,
         out_specs=(loose, vmem, vmem, vmem),
@@ -557,11 +559,11 @@
         key_matrix.T,
         value_matrix.T,
     )
-    done = (input_grad, key_sum, value_sum, gain_sum)
+    done = (input_grad, key_sum, value_sum, gain_sum, norm_gain.reshape(1, width))
     input_grad, key_sum, value_sum, gain_sum = pl.pallas_call(
-        hand_over,
-        out_shape=tuple(jax.ShapeDtypeStruct(a.shape, a.dtype) for a in done),
-        in_specs=[loose] + [vmem] * 3,
+        functools.partial(hand_over, scale),
+        out_shape=tuple(jax.ShapeDtypeStruct(a.shape, a.dtype) for a in done[:3] + done[4:]),
+        in_specs=[loose] + [vmem] * 4,
         out_specs=(loose,) + (vmem,) * 3,
         scratch_shapes=[pltpu.VMEM((rows, width), BF16), dma((SPLIT,)), dma((SPLIT,))],
     )(*done)

time: 76.8 us -> 72.2 us (0.940)
  Pallas kernels: 76 us -> 71.3 us
    pallas_call x1, Pallas kernels: 72.8 us -> 68.1 us  [per_device(): pl.pallas_call(functools.partial(kernel, scale), out_shape=(jax.ShapeDtyp...]
where the time goes in v3:
time: 72.2 us; the launch traced here: 71.9 us
  Pallas kernels  71.3 us (99%)
    pallas_call x1, Pallas kernels, per_device(): pl.pallas_call(functools.partial(kernel, scale), out_shape=(jax.ShapeDtyp...  68.1 us
    pallas_call x1, Pallas kernels, per_device(): pl.pallas_call(functools.partial(hand_over, scale), out_shape=tuple((jax....  3.18 us

profile of v3, /device:TPU:1, one launch (start us, length us, event | category | flops | bytes accessed | tf_op | source)
XLA Modules:
  0.0 71.9 jit_solution(3909466364635073107)
XLA Ops:
  0.6 68.1 %shard_map.102 = (bf16[128,2048]{1,0:T(8,128)(2,1)}, f32[32,64]{1,0:T(8,128)}, f32[32,64]{1,0:T(8,128)}, f32[8,1,256]{2,1,0:T(1,128)}) custom-call(bf16[128,2048]{1,0:T(8,128)(2,1)} %hid_hbm.1, f32[1,2048]{1,0:T(1,128)} %bitcast.10, bf16[128,2048]{1,0:T(8,128)(2,1)} %res_hbm.1, bf16[64,1024]{1,0:T(8,128)(2,1)} %bitcast.8, bf16[64,1024]{1,0:T(8,128)(2,1)} %bitcast.9, ...), custom_call_target="tpu_custom_call" | custom-call | tf_op jit(solution)/shard_map/pallas_call | solution.py:488
  68.8 3.2 %shard_map.103 = (bf16[128,2048]{1,0:T(8,128)(2,1)}, f32[32,64]{1,0:T(8,128)}, f32[32,64]{1,0:T(8,128)}, f32[1,2048]{1,0:T(1,128)}) custom-call(bf16[128,2048]{1,0:T(8,128)(2,1)} %get-tuple-element.12.grad, f32[32,64]{1,0:T(8,128)} %get-tuple-element.13.key, f32[32,64]{1,0:T(8,128)} %get-tuple-element.14.value, f32[8,1,256]{2,1,0:T(1,128)} %get-tuple-element.15.gain, ...), custom_call_target="tpu_custom_call" | custom-call | tf_op jit(solution)/shard_map/pallas_call | solution.py:563

commit v4 on v3

--- a/solution.py
+++ b/solution.py
@@ -12,7 +12,7 @@
 MESH = pl.DeviceIdType.MESH
 BF16, F32 = jnp.bfloat16, jnp.float32
 NX, NY, NZL, NZH, NC = 4, 4, 8, 2, 2
-SPLIT = 4
+SPLIT = 8
 NT_DIMS = (((1,), (1,)), ((), ()))
 
 
@@ -261,7 +261,6 @@
     n_core = go(remote(nt.at[(c + 1) % NC], ng_all.at[1, :, :, mine], n_s.at[4 * NY * NC], n_r.at[4 * NY * NC], device(dc=1)))
     own = pltpu.make_async_copy(nt.at[c], ng_all.at[0, :, :, mine], load_sem.at[9])
     own.start()
-    k_x = token_sends(0)
     n_direct.append(normed_sends(1))
 
     def y_sends(rel):
@@ -300,9 +299,9 @@
     ]
     n_pass = [normed_pass(0)]
     n_direct.append(normed_sends(2))
-    w_y3 = y_pass(0, w_y1)
     n_pass.append(normed_pass(1))
     n_direct.append(normed_sends(3))
+    w_y3 = y_pass(0, w_y1)
     for copy in w_z:
         copy.wait_recv()
     w_x2 = x_sends(1)
@@ -322,7 +321,6 @@
             device(dc=1),
         )
     )
-    k_x += token_sends(1)
 
     y_all = []
 
@@ -346,6 +344,8 @@
     weight_chunk(0)
     n_pass.append(normed_pass(2))
     weight_chunk(1)
+    k_x = token_sends(0)
+    k_x += token_sends(1)
     n_pass.append(normed_pass(3))
     weight_chunk(2)
     for copy in w_x2:
@@ -416,6 +416,22 @@
             inner = inner + jnp.sum(both * gain[:, here], axis=-1, keepdims=True)
     inner = inner * (1.0 / width)
 
+    for copy in z_all:
+        copy.wait_recv()
+    total = own_sum[aligned(zl, block), 0 : 2 * cols]
+    for i in range(nz - 1):
+        total = total + z_recv[i].astype(F32)
+    total = total * scale
+    kw_ref[...] = total[:, :cols]
+    vw_ref[...] = total[:, cols:]
+
+    for copy in g_3:
+        copy.wait_recv()
+    me = y * NC + c
+    gf[me] = jnp.sum(g3[...], axis=0)
+    g_4 = [
+        go(remote(gf.at[me], gf.at[me], g4_s.at[i], g4_r.at[i], device(dc=dc, dy=dy))) for i, (dy, dc) in enumerate(yc)
+    ]
     loads[8].wait()
     for at in range(0, width, chunk):
         here = slice(at, at + chunk)
@@ -425,22 +441,6 @@
     stores = [pltpu.make_async_copy(out_buf, out_ref, load_sem.at[10])]
     for store in stores:
         store.start()
-    for copy in z_all:
-        copy.wait_recv()
-    total = own_sum[aligned(zl, block), 0 : 2 * cols]
-    for i in range(nz - 1):
-        total = total + z_recv[i].astype(F32)
-    total = total * scale
-    kw_ref[...] = total[:, :cols]
-    vw_ref[...] = total[:, cols:]
-
-    for copy in g_3:
-        copy.wait_recv()
-    me = y * NC + c
-    gf[me] = jnp.sum(g3[...], axis=0)
-    g_4 = [
-        go(remote(gf.at[me], gf.at[me], g4_s.at[i], g4_r.at[i], device(dc=dc, dy=dy))) for i, (dy, dc) in enumerate(yc)
-    ]
     for copy in g_4:
         copy.wait_recv()
     gain_out[...] = gf[...]

time: 72.2 us -> 71.7 us (level)
  no operation moved by 1% of the time
where the time goes in v4:
time: 71.7 us; the launch traced here: 71.5 us
  Pallas kernels  70.8 us (99%)
    pallas_call x1, Pallas kernels, per_device(): pl.pallas_call(functools.partial(kernel, scale), out_shape=(jax.ShapeDtyp...  67.6 us
    pallas_call x1, Pallas kernels, per_device(): pl.pallas_call(functools.partial(hand_over, scale), out_shape=tuple((jax....  3.22 us

profile of v4, /device:TPU:1, one launch (start us, length us, event | category | flops | bytes accessed | tf_op | source)
XLA Modules:
  0.0 71.5 jit_solution(5748373263460269106)
XLA Ops:
  0.6 67.6 %shard_map.102 = (bf16[128,2048]{1,0:T(8,128)(2,1)}, f32[32,64]{1,0:T(8,128)}, f32[32,64]{1,0:T(8,128)}, f32[8,1,256]{2,1,0:T(1,128)}) custom-call(bf16[128,2048]{1,0:T(8,128)(2,1)} %hid_hbm.1, f32[1,2048]{1,0:T(1,128)} %bitcast.10, bf16[128,2048]{1,0:T(8,128)(2,1)} %res_hbm.1, bf16[64,1024]{1,0:T(8,128)(2,1)} %bitcast.8, bf16[64,1024]{1,0:T(8,128)(2,1)} %bitcast.9, ...), custom_call_target="tpu_custom_call" | custom-call | tf_op jit(solution)/shard_map/pallas_call | solution.py:488
  68.3 3.2 %shard_map.103 = (bf16[128,2048]{1,0:T(8,128)(2,1)}, f32[32,64]{1,0:T(8,128)}, f32[32,64]{1,0:T(8,128)}, f32[1,2048]{1,0:T(1,128)}) custom-call(bf16[128,2048]{1,0:T(8,128)(2,1)} %get-tuple-element.12.grad, f32[32,64]{1,0:T(8,128)} %get-tuple-element.13.key, f32[32,64]{1,0:T(8,128)} %get-tuple-element.14.value, f32[8,1,256]{2,1,0:T(1,128)} %get-tuple-element.15.gain, ...), custom_call_target="tpu_custom_call" | custom-call | tf_op jit(solution)/shard_map/pallas_call | solution.py:563
